TPU v7x, 512 devices: a whole 4x8x8 slice. The times are simulated.
512 devices in a mesh: segment: 4 (over z_lo), dp: 128 (over z_hi, y, x, core).
Axes of the slice: x: 4, y: 8, z: 8 (z_hi: 2, z_lo: 4; z = z_hi * 4 + z_lo), core: 2. Of those that a mesh axis runs over, the one named last changes fastest.
Arguments:
- hidden: bfloat16 [4, 256, 7168], P('segment', 'dp')
- head_weight: bfloat16 [65536, 7168], P(('segment', 'dp')), as said below
- target_ids: int32 [4, 256], P('segment', 'dp'), may hold values from 0 to 65535
- policy_logp: float32 [4, 256], P('segment', 'dp'), may hold values from -20 to -10
Outputs:
- ref_logp: float32 [4, 256], P('segment', 'dp')
- kl_term: float32 [4, 256], P('segment', 'dp')
Inputs may be any that keep to these rules, and one draw needn't show every extreme that they name: `head_weight`: each vocabulary row of the head is drawn on its own.
All inputs are finite; a program needn't handle non-finite values.
Results may differ from a plain program's by a relative error of at most 0.0006.
Values may be sent and summed in bfloat16 or wider, within the bound.
No kernel may reach another device: no remote copies, remote signals or barrier semaphores. Data moves between devices by JAX's collectives and lax.ppermute only.
A program may use at most 128 MiB of HBM per device.

v0:
```python
import jax
import jax.numpy as jnp
from jax import lax
from jax.sharding import PartitionSpec as P


def shifted(block, axis, distance):
    devices = range(lax.axis_size(axis))
    route = [((i - distance) % len(devices), i) for i in devices]
    return lax.ppermute(block, axis, route)


def local_stats(logits, columns, row_ids):
    maxima = jnp.max(logits, axis=-1)
    totals = jnp.sum(jnp.exp(logits - maxima[..., None]), axis=-1)
    picked = jnp.sum(jnp.where(row_ids[..., None] == columns, logits, 0.0), axis=-1)
    return (maxima, totals, picked)


def across_all(maxima, totals, picked):
    highest = lax.pmax(maxima, ("segment", "dp"))
    summed, gathered_pick = lax.psum(
        (totals * jnp.exp(maxima - highest), picked), ("segment", "dp")
    )
    merged = (highest, summed, gathered_pick)
    return merged


def finish(highest, totals, picked, policy_logp):
    ref_logp = picked - (highest + jnp.log(totals))
    log_ratio = ref_logp - policy_logp
    kl_term = jnp.minimum(jnp.exp(log_ratio) - log_ratio - 1.0, 10.0)
    return (ref_logp, kl_term)


def per_device(hidden, head_weight, target_ids, policy_logp):
    segment_count = lax.axis_size("segment")
    group_count = lax.axis_size("dp")
    segment_index = lax.axis_index("segment")
    group_index = lax.axis_index("dp")
    batches = hidden.shape[0]
    row_dev = hidden.shape[1]
    voc_dev = head_weight.shape[0]
    columns = (segment_index * group_count + group_index) * voc_dev + jnp.arange(
        voc_dev, dtype=jnp.int32
    )
    block, block_ids = (hidden, target_ids)
    shape_all = (batches * segment_count, row_dev * group_count)
    maxima = jnp.zeros(shape_all, jnp.float32)
    totals = jnp.zeros(shape_all, jnp.float32)
    picked = jnp.zeros(shape_all, jnp.float32)
    for offset in range(segment_count):
        if offset > 0:
            block, block_ids = shifted((block, block_ids), "segment", 1)
        gathered, gathered_ids = (
            lax.all_gather(block, "dp", axis=1, tiled=True),
            lax.all_gather(block_ids, "dp", axis=1, tiled=True),
        )
        logits = jnp.einsum(
            "grd,vd->grv", gathered, head_weight, preferred_element_type=jnp.float32
        )
        partial_value = local_stats(logits, columns, gathered_ids)
        anchor = (segment_index - offset) % segment_count * batches
        maxima = lax.dynamic_update_slice_in_dim(maxima, partial_value[0], anchor, 0)
        totals = lax.dynamic_update_slice_in_dim(totals, partial_value[1], anchor, 0)
        picked = lax.dynamic_update_slice_in_dim(picked, partial_value[2], anchor, 0)
    merged = across_all(maxima, totals, picked)
    first_batch = segment_index * batches
    merged = tuple((lax.dynamic_slice_in_dim(member, first_batch, batches, 0) for member in merged))
    first_row = group_index * row_dev
    highest, summed, chosen = tuple(
        (lax.dynamic_slice_in_dim(member, first_row, row_dev, 1) for member in merged)
    )
    return finish(highest, summed, chosen, policy_logp)


def solution(mesh):
    return jax.shard_map(
        per_device,
        mesh=mesh,
        in_specs=(
            P("segment", "dp", None),
            P(("segment", "dp"), None),
            P("segment", "dp"),
            P("segment", "dp"),
        ),
        out_specs=(P("segment", "dp"), P("segment", "dp")),
        check_vma=False,
    )
```

profile of v0, /device:TPU:1, one launch (start us, length us, event | category | flops | bytes accessed | tf_op | source)
XLA Modules:
  0.0 830.2 jit_solution(3139782764414474931)
XLA Ops:
  7.2 1.5 copy.8
  8.8 4.8 collective-permute-start.1
  13.7 5.4 collective-permute-done.1
  19.1 0.6 copy-done.1
  19.7 1.9 collective-permute-start.3
  21.7 5.0 collective-permute-done.3
  26.7 0.6 copy-done.2
  27.4 1.9 collective-permute-start.5
  29.3 5.0 collective-permute-done.5
  34.3 0.6 copy-done.3
  34.9 1.9 collective-permute-start
  36.9 1.3 dynamic-slice
  38.9 0.8 bitcast_dynamic-update-slice_fusion.3
  39.7 1.9 collective-permute-done
  41.5 1.9 collective-permute-start.2
  43.6 4.0 collective-permute-done.2
  47.6 1.9 collective-permute-start.4
  49.6 0.1 bitcast_dynamic-update-slice_fusion.1
  49.7 4.0 collective-permute-done.4
  53.8 32.7 %all-reduce.4 = (s32[256]{0:T(256)S(1)}, s32[256]{0:T(256)S(1)}, s32[256]{0:T(256)S(1)}, s32[256]{0:T(256)S(1)}) all-reduce(s32[256]{0:T(256)S(1)} %bitcast_dynamic-update-slice_fusion, s32[256]{0:T(256)S(1)} %bitcast_dynamic-update-slice_fusion.2, ...), channel_id=1, replica_groups=mesh['segment'=4,'dp'=128] {'dp'}, use_global_device_ids=true, to_apply=%add.3 | all-reduce | flops 1024 | bytes 8192
  86.5 85.5 %all-gather.5.cloned.1.call-done = bf16[1,256,7168]{2,0,1:T(2,128)(2,1)} async-done(((bf16[1,2,7168]{2,0,1:T(2,128)(2,1)}), bf16[1,256,7168]{2,0,1:T(2,128)(2,1)}) %all-gather.5.cloned.1.call-update) | async-done | bytes 3670032 | tf_op jit(solution)/shard_map/all_gather | solution.py:56
  172.1 4.6 fusion.17
  176.7 147.4 %all-gather.7.cloned.1.call-done = bf16[1,256,7168]{2,0,1:T(2,128)(2,1)} async-done(((bf16[1,2,7168]{2,0,1:T(2,128)(2,1)}), bf16[1,256,7168]{2,0,1:T(2,128)(2,1)}) %all-gather.7.cloned.1.call-update) | async-done | bytes 3670032 | tf_op jit(solution)/shard_map/all_gather | solution.py:56
  324.1 4.6 fusion.15
  328.8 147.4 %all-gather.9.cloned.1.call-done = bf16[1,256,7168]{2,0,1:T(2,128)(2,1)} async-done(((bf16[1,2,7168]{2,0,1:T(2,128)(2,1)}), bf16[1,256,7168]{2,0,1:T(2,128)(2,1)}) %all-gather.9.cloned.1.call-update) | async-done | bytes 3670032 | tf_op jit(solution)/shard_map/all_gather | solution.py:56
  476.2 4.6 fusion.16
  480.9 147.3 %all-gather.11.cloned.1.call-done = bf16[1,256,7168]{2,0,1:T(2,128)(2,1)} async-done(((bf16[1,2,7168]{2,0,1:T(2,128)(2,1)}), bf16[1,256,7168]{2,0,1:T(2,128)(2,1)}) %all-gather.11.cloned.1.call-update) | async-done | bytes 3670032 | tf_op jit(solution)/shard_map/all_gather | solution.py:56
  628.1 4.6 fusion.14
  632.8 96.2 %pmax.7 = f32[4,256]{1,0:T(4,128)S(1)} all-reduce(f32[4,256]{1,0:T(4,128)S(1)} %dynamic_update_slice.43), channel_id=1, replica_groups=mesh['segment'=4,'dp'=128] {'segment','dp'}, use_global_device_ids=true, to_apply=%region_9.10 | all-reduce | flops 1024 | bytes 8192 | tf_op jit(solution)/shard_map/pmax | solution.py:21
  729.0 0.2 select_reduce_fusion
  729.5 93.6 %all-reduce.5 = (f32[4,256]{1,0:T(4,128)S(1)}, f32[4,256]{1,0:T(4,128)S(1)}) all-reduce(f32[4,256]{1,0:T(4,128)S(1)} %exponential_multiply_fusion, f32[4,256]{1,0:T(4,128)S(1)} %dynamic_update_slice.39), channel_id=1, replica_groups=mesh['segment'=4,'dp'=128] {'segment','dp'}, use_global_device_ids=true, to_apply=%region_14.15 | all-reduce | flops 2048 | bytes 16384 | tf_op jit(solution)/shard_map/psum | solution.py:22
  823.1 0.6 fusion.13
  (38 shorter events, 1.0 us)
Async XLA Ops:
  7.2 164.9 %copy-start = (bf16[128,7168]{1,0:T(8,128)(2,1)S(1)}, bf16[128,7168]{1,0:T(8,128)(2,1)}, u32[]{:S(2)}) copy-start(bf16[128,7168]{1,0:T(8,128)(2,1)} %param.5) | copy-start | bytes 5505028
  7.2 164.9 %all-gather.5.cloned.1.call-start = ((), (), s32[]{:S(2)}) async-start(), calls=%async_computation | async-start | bytes 7397376 | tf_op jit(solution)/shard_map/all_gather | solution.py:56
  8.8 315.4 %all-gather.7.cloned.1.call-start = ((), (), s32[]{:S(2)}) async-start(), calls=%async_computation.1 | async-start | bytes 7397376 | tf_op jit(solution)/shard_map/all_gather | solution.py:56
  8.8 10.2 %collective-permute-start.1 = (bf16[1,2,7168]{2,0,1:T(2,128)(2,1)}, bf16[1,2,7168]{2,0,1:T(2,128)(2,1)S(1)}, u32[]{:S(2)}, u32[]{:S(2)}) collective-permute-start(bf16[1,2,7168]{2,0,1:T(2,128)(2,1)} %copy.8), channel_id=1, source_target_pairs={{384,0},{0,128},{128,256},{256,384},{385,1},{1,129},{129,257},{257... | collective-permute-start | bytes 86024 | tf_op jit(solution)/shard_map/ppermute | solution.py:10
  19.0 0.6 copy-start.1
  19.7 456.5 %all-gather.9.cloned.1.call-start = ((), (), s32[]{:S(2)}) async-start(), calls=%async_computation.2 | async-start | bytes 7397376 | tf_op jit(solution)/shard_map/all_gather | solution.py:56
  19.7 6.9 collective-permute-start.3
  26.7 0.6 copy-start.2
  27.3 600.8 %all-gather.11.cloned.1.call-start = ((), (), s32[]{:S(2)}) async-start(), calls=%async_computation.3 | async-start | bytes 7397376 | tf_op jit(solution)/shard_map/all_gather | solution.py:56
  27.4 6.9 collective-permute-start.5
  34.3 0.6 copy-start.3
  34.9 6.6 collective-permute-start
  41.5 6.1 collective-permute-start.2
  47.6 6.1 collective-permute-start.4
  480.8 342.3 %copy-start.4 = (f32[1,2]{1,0:T(1,128)S(1)}, f32[1,2]{1,0:T(1,128)}, u32[]{:S(2)}) copy-start(f32[1,2]{1,0:T(1,128)} %param.7) | copy-start | bytes 28
Sparse Core Ops, SparseCore 0:
  12.6 159.4 all-gather.4
  176.6 147.4 all-gather.6
  328.7 147.4 all-gather.8
  480.7 147.4 all-gather.10
where the time goes:
time: 831 us; the launch traced here: 830 us
  waiting for transfers between devices  553 us (67%)
  blocking collectives  223 us (27%)
  matrix products  18.3 us (2%)
  between operations  14.7 us (2%)
  starting transfers between devices  14.6 us (2%)
    all_gather x4, waiting for transfers between devices, per_device(): lax.all_gather(block, 'dp', axis=1, tiled=True)  528 us
    pmax x1, blocking collectives, across_all(): highest = lax.pmax(maxima, ('segment', 'dp'))  96.2 us
    psum x1, blocking collectives, across_all(): lax.psum((totals * jnp.exp(maxima - highest), picked), ('segment', 'dp'))  93.6 us
    unnamed x1, blocking collectives  32.7 us
    ppermute x6, waiting for transfers between devices, shifted(): return lax.ppermute(block, axis, route)  25.4 us
    dot_general x4, matrix products, per_device(): jnp.einsum('grd,vd->grv', gathered, head_weight, preferred_element_type=j...  18.3 us
  transfers between devices with their start and end apart: 10, of which 10 were waited for; matrix products, arithmetic and copies ran while one was open for 2% of the time, Pallas kernels for 0%

commit v1 on v0

--- a/solution.py
+++ b/solution.py
@@ -53,7 +53,9 @@
         if offset > 0:
             block, block_ids = shifted((block, block_ids), "segment", 1)
         gathered, gathered_ids = (
-            lax.all_gather(block, "dp", axis=1, tiled=True),
+            jnp.concatenate(
+                lax.all_to_all(jnp.stack([block] * lax.axis_size("dp")), "dp", 0, 0), axis=1
+            ),
             lax.all_gather(block_ids, "dp", axis=1, tiled=True),
         )
         logits = jnp.einsum(

time: 831 us -> 689 us (0.83)
  waiting for transfers between devices: 553 us -> 330 us
  local copies, waits for them, and re-layouts: 6.21 us -> 51.6 us
  starting transfers between devices: 14.6 us -> 55.1 us
  between operations: 14.7 us -> 1.6 us
  blocking collectives: 223 us -> 235 us
    all_gather x4 -> x0, waiting for transfers between devices: 528 us -> none  [per_device(): lax.all_gather(block, 'dp', axis=1, tiled=True)]
    ppermute x6, waiting for transfers between devices: 25.4 us -> 219 us  [shifted(): return lax.ppermute(block, axis, route)]
    all_to_all x0 -> x4, waiting for transfers between devices: none -> 111 us  [per_device(): lax.all_to_all(jnp.stack([block] * lax.axis_size('dp')), 'dp', 0, 0)]
    another operation x3 -> x11, local copies, waits for them, and re-layouts: 0.01 us -> 49.2 us
    all_to_all x0 -> x4, starting transfers between devices: none -> 42 us  [per_device(): lax.all_to_all(jnp.stack([block] * lax.axis_size('dp')), 'dp', 0, 0)]
    unnamed x1, blocking collectives: 32.7 us -> 41.2 us
  transfers between devices with their start and end apart: 10 -> 10, of which waited for: 10 -> 9; matrix products, arithmetic and copies ran while one was open for 2% -> 5% of each run, Pallas kernels for 0% -> 0%
where the time goes in v1:
time: 689 us; the launch traced here: 687 us
  waiting for transfers between devices  330 us (48%)
  blocking collectives  235 us (34%)
  starting transfers between devices  55.1 us (8%)
  local copies, waits for them, and re-layouts  51.6 us (7%)
  matrix products  13.6 us (2%)
    ppermute x6, waiting for transfers between devices, shifted(): return lax.ppermute(block, axis, route)  219 us
    all_to_all x4, waiting for transfers between devices, per_device(): lax.all_to_all(jnp.stack([block] * lax.axis_size('dp')), 'dp', 0, 0)  111 us
    pmax x1, blocking collectives, across_all(): highest = lax.pmax(maxima, ('segment', 'dp'))  98.9 us
    psum x1, blocking collectives, across_all(): lax.psum((totals * jnp.exp(maxima - highest), picked), ('segment', 'dp'))  94.5 us
    all_to_all x4, starting transfers between devices, per_device(): lax.all_to_all(jnp.stack([block] * lax.axis_size('dp')), 'dp', 0, 0)  42 us
    unnamed x1, blocking collectives  41.2 us
    another operation x7, local copies, waits for them, and re-layouts  33.6 us
    another operation x4, local copies, waits for them, and re-layouts, per_device(): jnp.stack([block] * lax.axis_size('dp'))  15.6 us
  transfers between devices with their start and end apart: 10, of which 9 were waited for; matrix products, arithmetic and copies ran while one was open for 5% of the time, Pallas kernels for 0%

profile of v1, /device:TPU:1, one launch (start us, length us, event | category | flops | bytes accessed | tf_op | source)
XLA Modules:
  0.0 687.4 jit_solution(47034328517952190)
XLA Ops:
  0.6 4.6 stack.8
  5.2 21.4 %all-to-all-start = ((bf16[128,1,2,7168]{3,2,1,0:T(2,128)(2,1)}), bf16[128,1,2,7168]{3,2,1,0:T(2,128)(2,1)}, u32[]{:S(2)}, u32[]{:S(2)}) async-start(bf16[128,1,2,7168]{3,2,1,0:T(2,128)(2,1)} %stack.8), calls=%async_computation | async-start | bytes 7340032 | tf_op jit(solution)/shard_map/all_to_all | solution.py:57
  26.6 3.1 collective-permute-start.1
  29.7 28.2 %collective-permute-done.1 = bf16[1,2,7168]{2,1,0:T(2,128)(2,1)S(1)} collective-permute-done((bf16[1,2,7168]{2,1,0:T(2,128)(2,1)S(1)}, bf16[1,2,7168]{2,1,0:T(2,128)(2,1)S(1)}, u32[]{:S(2)}, u32[]{:S(2)}) %collective-permute-start.1) | collective-permute-done | bytes 28704 | tf_op jit(solution)/shard_map/ppermute | solution.py:10
  57.9 59.3 %all-to-all-done = bf16[128,1,2,7168]{3,2,1,0:T(2,128)(2,1)} async-done(((bf16[128,1,2,7168]{3,2,1,0:T(2,128)(2,1)}), bf16[128,1,2,7168]{3,2,1,0:T(2,128)(2,1)}, u32[]{:S(2)}, u32[]{:S(2)}) %all-to-all-start) | async-done | bytes 3670048 | tf_op jit(solution)/shard_map/all_to_all | solution.py:57
  117.2 3.7 stack.9
  120.9 7.2 %all-to-all-start.1 = ((bf16[128,1,2,7168]{3,2,1,0:T(2,128)(2,1)}), bf16[128,1,2,7168]{3,2,1,0:T(2,128)(2,1)}, u32[]{:S(2)}, u32[]{:S(2)}) async-start(bf16[128,1,2,7168]{3,2,1,0:T(2,128)(2,1)} %stack.9), calls=%async_computation.1 | async-start | bytes 7340032 | tf_op jit(solution)/shard_map/all_to_all | solution.py:57
  128.1 2.4 collective-permute-start.3
  130.4 62.4 %collective-permute-done.3 = bf16[1,2,7168]{2,1,0:T(2,128)(2,1)S(1)} collective-permute-done((bf16[1,2,7168]{2,1,0:T(2,128)(2,1)S(1)}, bf16[1,2,7168]{2,1,0:T(2,128)(2,1)S(1)}, u32[]{:S(2)}, u32[]{:S(2)}) %collective-permute-start.3) | collective-permute-done | bytes 28704 | tf_op jit(solution)/shard_map/ppermute | solution.py:10
  192.8 25.9 %all-to-all-done.1 = bf16[128,1,2,7168]{3,2,1,0:T(2,128)(2,1)} async-done(((bf16[128,1,2,7168]{3,2,1,0:T(2,128)(2,1)}), bf16[128,1,2,7168]{3,2,1,0:T(2,128)(2,1)}, u32[]{:S(2)}, u32[]{:S(2)}) %all-to-all-start.1) | async-done | bytes 3670048 | tf_op jit(solution)/shard_map/all_to_all | solution.py:57
  218.7 3.7 stack.10
  222.4 6.8 all-to-all-start.2
  229.2 1.9 collective-permute-start.5
  231.1 62.5 %collective-permute-done.5 = bf16[1,2,7168]{2,1,0:T(2,128)(2,1)S(1)} collective-permute-done((bf16[1,2,7168]{2,1,0:T(2,128)(2,1)S(1)}, bf16[1,2,7168]{2,1,0:T(2,128)(2,1)S(1)}, u32[]{:S(2)}, u32[]{:S(2)}) %collective-permute-start.5) | collective-permute-done | bytes 28704 | tf_op jit(solution)/shard_map/ppermute | solution.py:10
  293.6 26.2 %all-to-all-done.2 = bf16[128,1,2,7168]{3,2,1,0:T(2,128)(2,1)} async-done(((bf16[128,1,2,7168]{3,2,1,0:T(2,128)(2,1)}), bf16[128,1,2,7168]{3,2,1,0:T(2,128)(2,1)}, u32[]{:S(2)}, u32[]{:S(2)}) %all-to-all-start.2) | async-done | bytes 3670048 | tf_op jit(solution)/shard_map/all_to_all | solution.py:57
  319.8 3.7 stack.11
  323.5 6.6 all-to-all-start.3
  330.1 1.9 collective-permute-start
  334.2 56.5 %collective-permute-done = s32[1,2]{1,0:T(1,128)S(1)} collective-permute-done((s32[1,2]{1,0:T(1,128)S(1)}, s32[1,2]{1,0:T(1,128)S(1)}, u32[]{:S(2)}, u32[]{:S(2)}) %collective-permute-start) | collective-permute-done | bytes 40 | tf_op jit(solution)/shard_map/ppermute | solution.py:10
  392.7 4.5 collective-permute-done.2
  399.2 4.8 collective-permute-done.4
  404.0 41.2 %all-reduce.4 = (s32[256]{0:T(256)S(1)}, s32[256]{0:T(256)S(1)}, s32[256]{0:T(256)S(1)}, s32[256]{0:T(256)S(1)}) all-reduce(s32[256]{0:T(256)S(1)} %bitcast_dynamic-update-slice_fusion, s32[256]{0:T(256)S(1)} %bitcast_dynamic-update-slice_fusion.2, ...), channel_id=1, replica_groups=mesh['segment'=4,'dp'=128] {'dp'}, use_global_device_ids=true, to_apply=%add.3 | all-reduce | flops 1024 | bytes 8192
  445.2 8.4 %reshape.102 = bf16[256,7168]{1,0:T(8,128)(2,1)} reshape(bf16[128,1,2,7168]{3,2,1,0:T(2,128)(2,1)} %all-to-all-done) | data formatting | bytes 7340032 | tf_op jit(solution)/shard_map/reshape.3
  453.6 3.4 fusion.5
  457.0 8.4 %reshape.103 = bf16[256,7168]{1,0:T(8,128)(2,1)} reshape(bf16[128,1,2,7168]{3,2,1,0:T(2,128)(2,1)} %all-to-all-done.1) | data formatting | bytes 7340032 | tf_op jit(solution)/shard_map/reshape.14
  465.4 3.4 fusion.3
  469.1 8.4 %reshape.104 = bf16[256,7168]{1,0:T(8,128)(2,1)} reshape(bf16[128,1,2,7168]{3,2,1,0:T(2,128)(2,1)} %all-to-all-done.2) | data formatting | bytes 7340032 | tf_op jit(solution)/shard_map/reshape.18
  477.5 3.4 fusion.4
  481.0 8.4 %reshape.105 = bf16[256,7168]{1,0:T(8,128)(2,1)} reshape(bf16[128,1,2,7168]{3,2,1,0:T(2,128)(2,1)} %all-to-all-done.3) | data formatting | bytes 7340032 | tf_op jit(solution)/shard_map/reshape.22
  489.4 3.4 fusion.2
  492.8 98.9 %pmax.7 = f32[4,256]{1,0:T(4,128)S(1)} all-reduce(f32[4,256]{1,0:T(4,128)S(1)} %dynamic_update_slice.43), channel_id=1, replica_groups=mesh['segment'=4,'dp'=128] {'segment','dp'}, use_global_device_ids=true, to_apply=%region_9.10 | all-reduce | flops 1024 | bytes 8192 | tf_op jit(solution)/shard_map/pmax | solution.py:21
  592.2 94.5 %all-reduce.5 = (f32[4,256]{1,0:T(4,128)S(1)}, f32[4,256]{1,0:T(4,128)S(1)}) all-reduce(f32[4,256]{1,0:T(4,128)S(1)} %exponential_multiply_fusion, f32[4,256]{1,0:T(4,128)S(1)} %dynamic_update_slice.39), channel_id=1, replica_groups=mesh['segment'=4,'dp'=128] {'segment','dp'}, use_global_device_ids=true, to_apply=%region_14.15 | all-reduce | flops 2048 | bytes 16384 | tf_op jit(solution)/shard_map/psum | solution.py:22
  (39 shorter events, 7.0 us)
Async XLA Ops:
  0.6 452.9 %copy-start = (bf16[128,7168]{1,0:T(8,128)(2,1)S(1)}, bf16[128,7168]{1,0:T(8,128)(2,1)}, u32[]{:S(2)}) copy-start(bf16[128,7168]{1,0:T(8,128)(2,1)} %param.5) | copy-start | bytes 5505028
  5.2 21.4 %copy-start.1 = (bf16[1,2,7168]{2,1,0:T(2,128)(2,1)S(1)}, bf16[1,2,7168]{2,1,0:T(2,128)(2,1)}, u32[]{:S(2)}) copy-start(bf16[1,2,7168]{2,1,0:T(2,128)(2,1)} %param.4) | copy-start | bytes 86020
  5.2 112.0 %all-to-all-start = ((bf16[128,1,2,7168]{3,2,1,0:T(2,128)(2,1)}), bf16[128,1,2,7168]{3,2,1,0:T(2,128)(2,1)}, u32[]{:S(2)}, u32[]{:S(2)}) async-start(bf16[128,1,2,7168]{3,2,1,0:T(2,128)(2,1)} %stack.8), calls=%async_computation | async-start | bytes 7340032 | tf_op jit(solution)/shard_map/all_to_all | solution.py:57
  26.6 31.3 %collective-permute-start.1 = (bf16[1,2,7168]{2,1,0:T(2,128)(2,1)S(1)}, bf16[1,2,7168]{2,1,0:T(2,128)(2,1)S(1)}, u32[]{:S(2)}, u32[]{:S(2)}) collective-permute-start(bf16[1,2,7168]{2,1,0:T(2,128)(2,1)S(1)} %copy-done.1), channel_id=1, source_target_pairs={{384,0},{0,128},{128,256},{256,384},{385,1},{1,129},{129,257},{257... | collective-permute-start | bytes 86024 | tf_op jit(solution)/shard_map/ppermute | solution.py:10
  120.9 97.8 %all-to-all-start.1 = ((bf16[128,1,2,7168]{3,2,1,0:T(2,128)(2,1)}), bf16[128,1,2,7168]{3,2,1,0:T(2,128)(2,1)}, u32[]{:S(2)}, u32[]{:S(2)}) async-start(bf16[128,1,2,7168]{3,2,1,0:T(2,128)(2,1)} %stack.9), calls=%async_computation.1 | async-start | bytes 7340032 | tf_op jit(solution)/shard_map/all_to_all | solution.py:57
  128.1 64.7 %collective-permute-start.3 = (bf16[1,2,7168]{2,1,0:T(2,128)(2,1)S(1)}, bf16[1,2,7168]{2,1,0:T(2,128)(2,1)S(1)}, u32[]{:S(2)}, u32[]{:S(2)}) collective-permute-start(bf16[1,2,7168]{2,1,0:T(2,128)(2,1)S(1)} %collective-permute-done.1), channel_id=1, source_target_pairs={{384,0},{0,128},{128,256},{256,384},{385,1},{1,129},{129,257},{257... | collective-permute-start | bytes 86024 | tf_op jit(solution)/shard_map/ppermute | solution.py:10
  222.4 97.4 %all-to-all-start.2 = ((bf16[128,1,2,7168]{3,2,1,0:T(2,128)(2,1)}), bf16[128,1,2,7168]{3,2,1,0:T(2,128)(2,1)}, u32[]{:S(2)}, u32[]{:S(2)}) async-start(bf16[128,1,2,7168]{3,2,1,0:T(2,128)(2,1)} %stack.10), calls=%async_computation.2 | async-start | bytes 7340032 | tf_op jit(solution)/shard_map/all_to_all | solution.py:57
  229.2 64.4 %collective-permute-start.5 = (bf16[1,2,7168]{2,1,0:T(2,128)(2,1)S(1)}, bf16[1,2,7168]{2,1,0:T(2,128)(2,1)S(1)}, u32[]{:S(2)}, u32[]{:S(2)}) collective-permute-start(bf16[1,2,7168]{2,1,0:T(2,128)(2,1)S(1)} %collective-permute-done.3), channel_id=1, source_target_pairs={{384,0},{0,128},{128,256},{256,384},{385,1},{1,129},{129,257},{257... | collective-permute-start | bytes 86024 | tf_op jit(solution)/shard_map/ppermute | solution.py:10
  323.5 6.6 copy-start.3
  323.5 157.5 %all-to-all-start.3 = ((bf16[128,1,2,7168]{3,2,1,0:T(2,128)(2,1)}), bf16[128,1,2,7168]{3,2,1,0:T(2,128)(2,1)}, u32[]{:S(2)}, u32[]{:S(2)}) async-start(bf16[128,1,2,7168]{3,2,1,0:T(2,128)(2,1)} %stack.11), calls=%async_computation.3 | async-start | bytes 7340032 | tf_op jit(solution)/shard_map/all_to_all | solution.py:57
  330.1 60.5 %collective-permute-start = (s32[1,2]{1,0:T(1,128)S(1)}, s32[1,2]{1,0:T(1,128)S(1)}, u32[]{:S(2)}, u32[]{:S(2)}) collective-permute-start(s32[1,2]{1,0:T(1,128)S(1)} %copy-done.3), channel_id=1, source_target_pairs={{384,0},{0,128},{128,256},{256,384},{385,1},{1,129},{129,257},{257... | collective-permute-start | bytes 32 | tf_op jit(solution)/shard_map/ppermute | solution.py:10
  390.6 6.5 collective-permute-start.2
  397.1 6.8 collective-permute-start.4
  489.4 197.4 %copy-start.2 = (f32[1,2]{1,0:T(1,128)S(1)}, f32[1,2]{1,0:T(1,128)}, u32[]{:S(2)}) copy-start(f32[1,2]{1,0:T(1,128)} %param.7) | copy-start | bytes 28
